TPU v7x, 512 devices: a whole 4x8x8 slice. The times are simulated.
512 devices in a mesh: grp: 32 (over x, y), seq: 16 (over z, core).
Axes of the slice: x: 4, y: 8, z: 8, core: 2. Of those that a mesh axis runs over, the one named last changes fastest.
Arguments:
- tokens: bfloat16 [131072, 512], P(('grp', 'seq')), parts along dimension 0, may hold values from -6 to 6
- group_pos: int32 [32768], P('grp'), parts along dimension 0, may hold values from 0 to 4095, as said below
- log_decay: float32 [131072, 16], P(('grp', 'seq')), parts along dimension 0, may hold values from -1 to 0, as said below
- in_weight: bfloat16 [512, 2176], replicated, may hold values from -0.25 to 0.25
- norm_gain: float32 [1024], replicated, may hold values from 0.1 to 1.9
- out_weight: bfloat16 [1024, 512], replicated, may hold values from -0.1875 to 0.1875
- inner_gain: float32 [512], replicated, may hold values from 0.1 to 1.9
- qkv_weight: bfloat16 [16, 512, 192], P('seq'), may hold values from -1 to 1
- attn_out: bfloat16 [16, 64, 512], P('seq'), may hold values from -0.1875 to 0.1875
Outputs:
- result: bfloat16 [131072, 512], P(('grp', 'seq')), parts along dimension 0
There are 32 independent parts, one for each index of `grp`. A program takes and returns all parts, laid end to end along the dimension named above; an argument that names none is the same for every part. Nothing has to cross between parts.
Inputs may be any that keep to these rules, and one draw needn't show every extreme that they name: `group_pos`: strictly increasing. Each device's 256 positions hold at least one group start and at most 128; some device holds exactly 128. `log_decay`: negative at every position.
All inputs are finite; a program needn't handle non-finite values.
Results may differ from a plain program's by a relative error of at most 0.0061.
Values may be sent and summed in bfloat16 or wider, within the bound.
A program may use at most 64 MiB of HBM per device.

v0:
```python
import jax
import jax.numpy as jnp
from jax import lax
from jax.sharding import Mesh
from jax.sharding import PartitionSpec as P

SEQ = ("seq_0", "seq_1")
GRP_SEQ = ("grp", "seq_0", "seq_1")


def nothing_yet(shard, identity):
    return jax.tree.map(
        lambda part, zero: jnp.zeros_like(part) + jnp.asarray(zero, part.dtype), shard, identity
    )


def carried_in(shard, axes, combine, identity):
    before = start = nothing_yet(shard, identity)
    subtotal = shard
    for axis in reversed(axes):
        count, here = (lax.axis_size(axis), lax.axis_index(axis))
        pieces = jax.tree.map(lambda part: lax.all_gather(part, axis), subtotal)
        inside, subtotal = (start, start)
        for k in range(count):
            passed = k < here
            subtotal = combine(subtotal, jax.tree.map(lambda part: part[k], pieces))
            inside = jax.tree.map(lambda new, old: jnp.where(passed, new, old), subtotal, inside)
        before = combine(inside, before)
    return before


def in_blocks(shard, dim, count):
    lengths = shard.shape
    tiles = shard.reshape(*lengths[:dim], count, lengths[dim] // count, *lengths[dim + 1 :])
    return jnp.moveaxis(tiles, dim, 0)


def joined_along(tiles, dim):
    tiles = jnp.moveaxis(tiles, 0, dim)
    lengths = tiles.shape
    return tiles.reshape(*lengths[:dim], lengths[dim] * lengths[dim + 1], *lengths[dim + 2 :])


def turned_blocks(tiles, axes, order):
    inside = tiles.shape[1:]
    result = tiles.reshape(*(lax.axis_size(a) for a in axes), *inside)
    for k in order:
        result = lax.all_to_all(result, axes[k], k, k, tiled=True)
    return result.reshape(-1, *inside)


def stepwise_exchange(shard, axes, order, split_dim, concat_dim):
    tiles = in_blocks(shard, split_dim, lax.axis_size(axes))
    return joined_along(turned_blocks(tiles, axes, order), concat_dim)


def rms_norm(values, gain):
    return values * lax.rsqrt(jnp.mean(values * values, axis=-1, keepdims=True) + 1e-05) * gain


def attend(rows, w_qkv, index, valid):
    head_dim = w_qkv.shape[1] // 3
    qkv = jnp.dot(rows, w_qkv, preferred_element_type=jnp.float32).astype(jnp.bfloat16)
    query = qkv[:, :head_dim]
    keys = qkv[:, head_dim : 2 * head_dim]
    values = qkv[:, 2 * head_dim :]
    count = rows.shape[0]
    block = min(512, count)

    def one_block(start):
        query_block = lax.dynamic_slice_in_dim(query, start, block, 0)
        index_block = lax.dynamic_slice_in_dim(index, start, block, 0)
        scores = jnp.dot(query_block, keys.T, preferred_element_type=jnp.float32) * head_dim ** (
            -0.5
        )
        allowed = (index[None, :] <= index_block[:, None]) & valid[None, :]
        scores = jnp.where(allowed, scores, -jnp.inf)
        top = jnp.max(scores, axis=1, keepdims=True)
        expo = jnp.exp(scores - top)
        probs = (expo / jnp.sum(expo, axis=1, keepdims=True)).astype(jnp.bfloat16)
        return jnp.dot(probs, values, preferred_element_type=jnp.float32).astype(jnp.bfloat16)

    starts = jnp.arange(count // block, dtype=jnp.int32) * block
    return lax.map(one_block, starts).reshape(count, head_dim)


def shards(
    tokens, group_pos, log_decay, in_weight, norm_gain, out_weight, inner_gain, qkv_weight, attn_out
):
    highest = lax.Precision.HIGHEST
    length = tokens.shape[0]
    heads = log_decay.shape[1]
    width = out_weight.shape[0]
    model_width = out_weight.shape[1]
    head_size = width // heads
    state_dim = (in_weight.shape[1] - 2 * width) // 2
    proj = jnp.dot(tokens, in_weight, preferred_element_type=jnp.float32).astype(jnp.bfloat16)
    xs = proj[:, :width].astype(jnp.float32).reshape(length, heads, head_size)
    gate = proj[:, width : 2 * width].astype(jnp.float32)
    bmat = proj[:, 2 * width : 2 * width + state_dim].astype(jnp.float32)
    cmat = proj[:, 2 * width + state_dim :].astype(jnp.float32)
    cumul = jnp.cumsum(log_decay, axis=0)
    differ = cumul.T[:, :, None] - cumul.T[:, None, :]
    lower = jnp.arange(length)[:, None] >= jnp.arange(length)[None, :]
    decays = jnp.exp(jnp.where(lower[None], differ, -jnp.inf))
    intersections = jnp.dot(cmat, bmat.T, precision=highest)
    within = jnp.einsum("hij,jhp->ihp", decays * intersections[None], xs, precision=highest)
    tails = jnp.exp(cumul[-1][None, :] - cumul)
    local_state = jnp.einsum("jh,jhp,jn->hpn", tails, xs, bmat, precision=highest)
    total_decay = jnp.exp(cumul[-1])

    def link(earlier, later):
        return (earlier[0] * later[0], later[0][:, None, None] * earlier[1] + later[1])

    identity = (jnp.ones_like(total_decay), jnp.zeros_like(local_state))
    _, state_in = carried_in((total_decay, local_state), SEQ, link, identity)
    carried = jnp.einsum("ih,in,hpn->ihp", jnp.exp(cumul), cmat, state_in, precision=highest)
    gated = (within + carried).reshape(length, width) * jax.nn.silu(gate)
    normed = rms_norm(gated, norm_gain).astype(jnp.bfloat16)
    hidden = (
        tokens.astype(jnp.float32) + jnp.dot(normed, out_weight, preferred_element_type=jnp.float32)
    ).astype(jnp.bfloat16)
    position = lax.axis_index(SEQ)
    devices = lax.axis_size(SEQ)
    most = length // 2
    groups = group_pos.shape[0]
    starts = jnp.arange(devices, dtype=jnp.int32) * length
    before = jnp.sum((group_pos[None, :] < starts[:, None]).astype(jnp.int32), axis=1)
    upto = jnp.sum((group_pos[None, :] < (starts + length)[:, None]).astype(jnp.int32), axis=1)
    counts = upto - before
    slots = jnp.arange(most, dtype=jnp.int32)
    picks = jnp.clip(before[position] + slots, 0, groups - 1)
    valid_here = slots < counts[position]
    local_pos = group_pos[picks] - position * length
    placing = (
        (local_pos[:, None] == jnp.arange(length, dtype=jnp.int32)[None, :]) & valid_here[:, None]
    ).astype(jnp.float32)
    rows = jnp.dot(placing.astype(jnp.bfloat16), hidden, preferred_element_type=jnp.float32)
    rows_n = rms_norm(rows, inner_gain).astype(jnp.bfloat16)
    gathered = lax.all_gather(rows_n, SEQ, axis=0, tiled=True)
    slot_group = (before[:, None] + slots[None, :]).reshape(-1)
    slot_valid = (slots[None, :] < counts[:, None]).reshape(-1)
    w_qkv = qkv_weight[0]
    owners = group_pos // length
    ordinal = jnp.arange(groups, dtype=jnp.int32)
    index = owners * most + ordinal - before[owners]
    packed = jnp.take(gathered, index, axis=0)
    outputs = attend(packed, w_qkv, ordinal, jnp.ones((groups,), jnp.bool_))
    spread = jnp.take(outputs, jnp.clip(slot_group, 0, groups - 1), axis=0)
    heads_out = jnp.where(slot_valid[:, None], spread, jnp.zeros_like(spread))
    full_out = lax.all_gather(attn_out, SEQ, axis=0, tiled=True)
    mine = stepwise_exchange(heads_out[:, None, :], SEQ, (1, 0), 0, 1)
    back = jnp.dot(
        mine.reshape(most, -1),
        full_out.reshape(-1, model_width),
        preferred_element_type=jnp.float32,
    )
    placed = jnp.dot(placing.T, back, precision=highest)
    return (hidden.astype(jnp.float32) + placed).astype(jnp.bfloat16)


def solution(mesh):
    split = Mesh(mesh.devices.reshape(mesh.shape["grp"], 8, 2), ("grp", "seq_0", "seq_1"))
    return jax.shard_map(
        shards,
        mesh=split,
        in_specs=(
            P(GRP_SEQ, None),
            P("grp"),
            P(GRP_SEQ, None),
            P(),
            P(),
            P(),
            P(),
            P(SEQ, None, None),
            P(SEQ, None, None),
        ),
        out_specs=P(GRP_SEQ, None),
        check_vma=False,
    )
```

profile of v0, /device:TPU:1, one launch (start us, length us, event | category | flops | bytes accessed | tf_op | source)
XLA Modules:
  0.0 190.4 jit_solution(11118988941506550398)
XLA Ops:
  6.5 1.6 copy-done
  8.2 2.0 %convolution_convert_fusion.1 = bf16[256,2176]{0,1:T(8,128)(2,1)S(1)} fusion(bf16[256,512]{1,0:T(8,128)(2,1)} %param.11, bf16[512,2176]{1,0:T(8,128)(2,1)S(1)} %copy-done), kind=kOutput, calls=%fused_computation.17 | convolution fusion | flops 570982400 | bytes 3604480 | tf_op jit(solution)/shard_map/dot_general | solution.py:97
  10.1 0.8 slice.156
  12.1 1.7 fusion.26
  13.8 9.2 %all-gather = f32[32,64,64]{2,1,0:T(8,128)} all-gather(f32[16,64,64]{2,1,0:T(8,128)S(1)} %fusion.26), channel_id=2, replica_groups=mesh['grp'=32,'seq_0'=8,'seq_1'=2] {'seq_1'}, dimensions={0}, use_global_device_ids=true | all-gather | bytes 786432 | tf_op jit(solution)/shard_map/all_gather | solution.py:22
  23.0 1.8 all-gather.1
  24.8 2.1 %bitcast_add_fusion = f32[1,16,64,64]{3,2,1,0:T(8,128)} fusion(f32[32,64,64]{2,1,0:T(8,128)} %all-gather, f32[16]{0:T(128)S(1)} %get-tuple-element.146, f32[16]{0:T(128)S(1)} %get-tuple-element.148), kind=kLoop, calls=%fused_computation.64 | loop fusion | flops 196608 | bytes 786560 | tf_op jit(solution)/shard_map/add | solution.py:113
  27.3 0.7 fusion.129
  28.7 1.0 gather_fusion
  30.3 13.1 %all-gather.2 = f32[8,1,16]{2,1,0:T(1,128)S(1)} all-gather(f32[1,1,16]{2,1,0:T(1,128)S(1)} %get-tuple-element.147), channel_id=1, replica_groups=mesh['grp'=32,'seq_0'=8,'seq_1'=2] {'seq_0'}, dimensions={0}, use_global_device_ids=true | all-gather | bytes 576 | tf_op jit(solution)/shard_map/all_gather | solution.py:22
  44.3 5.4 %fusion.15 = f32[256,16,64]{0,2,1:T(8,128)} fusion(bf16[256,16,64]{0,2,1:T(8,128)(2,1)} %bitcast.189, f32[256,256]{1,0:T(8,128)S(1)} %fusion.110, f32[16,256]{1,0:T(8,128)S(1)} %get-tuple-element.136, pred[256,256]{1,0:T(8,128)(4,1)S(1)} %iota_compare_fusion), kind=kOutput, calls=%fused_computation.23 | convolution fusion | flops 808452096 | bytes 1916928 | tf_op jit(solution)/shard_map/hij,jhp->ihp/dot_general | solution.py:107
  49.7 34.7 %all-gather.7.cloned.1.call-done = f32[8,16,64,64]{3,2,1,0:T(8,128)} async-done(((f32[1,16,64,64]{3,2,1,0:T(8,128)}), f32[8,16,64,64]{3,2,1,0:T(8,128)}) %all-gather.7.cloned.1.call-update) | async-done | bytes 2097168 | tf_op jit(solution)/shard_map/all_gather | solution.py:22
  84.3 4.5 %fusion.18 = f32[256,16,64]{0,2,1:T(8,128)S(1)} fusion(f32[256,16,64]{0,2,1:T(8,128)} %fusion.15, f32[8,16,64,64]{3,2,1,0:T(8,128)} %all-gather.7.cloned.1.call-done, f32[256,16]{0,1:T(8,128)S(1)} %get-tuple-element.133, f32[256,64]{0,1:T(8,128)S(1)} %slice_convert_fusion, f32[32,64,64]{2,1,0:T(8,128)} %all-gather, f32[16]{0:T(128)S(1)} %get-tuple-element.146, ...), kind=kOutput, calls=%fused_computation.25 | convolution fusion | flops 203816960 | bytes 4801226 | tf_op jit(solution)/shard_map/ih,in,hpn->ihp/dot_general | solution.py:117
  90.2 0.8 fusion.19
  91.3 0.8 multiply_convert_fusion.2
  92.1 0.7 all-gather.11.cloned.1.call-update
  93.1 10.1 %compare_and_fusion = (pred[1024]{0:T(1024)(128)(4,1)S(1)}, s32[1024]{0:T(1024)S(1)}) fusion(s32[]{:T(128)} %bitcast.45, s32[]{:T(128)} %bitcast.44, s32[]{:T(128)} %bitcast.43, s32[]{:T(128)} %bitcast.42, s32[]{:T(128)} %bitcast.41, s32[]{:T(128)} %bitcast.40, s32[]{:T(128)} %bitcast.39, s32[]{:T(128)} %bitcast.38, s32[]{:T(128)} %bitcast.37, s32[]{:T(128)} %bitcast.36, ...), kind=kLoop, calls=%fused_computation.165 | loop fusion | flops 58368 | bytes 9280 | tf_op jit(solution)/shard_map/jit(_take)/and | solution.py:147
  103.6 30.4 %all-gather.9.cloned.1.call-done = bf16[2048,512]{1,0:T(8,128)(2,1)} async-done(((bf16[128,512]{1,0:T(8,128)(2,1)}), bf16[2048,512]{1,0:T(8,128)(2,1)}) %all-gather.9.cloned.1.call-update) | async-done | bytes 2097168 | tf_op jit(solution)/shard_map/all_gather | solution.py:140
  134.0 7.0 %gather_fusion.1 = bf16[1024,512]{1,0:T(8,128)(2,1)} fusion(bf16[2048,512]{1,0:T(8,128)(2,1)} %all-gather.9.cloned.1.call-done, s32[1024]{0:T(1024)S(1)} %broadcast_clamp_fusion.1), kind=kCustom, calls=%fused_computation.1 | custom fusion | bytes 2101248 | tf_op jit(solution)/shard_map/jit(_take)/gather | solution.py:147
  140.9 1.8 convolution_convert_fusion.2
  142.7 0.7 fusion.128
  143.8 11.1 %while.11 = (s32[]{:T(128)}, bf16[2,512,64]{1,2,0:T(8,128)(2,1)S(1)}, s32[1024]{0:T(1024)S(1)}, s32[2]{0:T(128)S(1)}, bf16[1024,64]{0,1:T(8,128)(2,1)}, /*index=...) while((s32[]{:T(128)}, ...), condition=%wide.region_9.10_spmd.clone, body=%wide.region_6.9_spmd.clone.sunk | while | flops 138968064 | bytes 6836391 | solution.py:84
  146.6 1.6 fusion.149
  152.2 1.6 fusion.149
  155.1 6.2 %gather_fusion.2 = bf16[2048,64]{1,0:T(8,128)(2,1)S(1)} fusion(bf16[1024,64]{1,0:T(8,128)(2,1)S(1)} %bitcast.186, s32[2048]{0:T(1024)S(1)} %broadcast_clamp_fusion), kind=kCustom, calls=%fused_computation.2 | custom fusion | bytes 532480 | tf_op jit(solution)/shard_map/jit(_take)/gather | solution.py:149
  161.6 3.8 %all_to_all.10 = bf16[8,2,128,1,64]{2,4,3,0,1:T(8,128)(2,1)S(1)} all-to-all(bf16[8,2,128,1,64]{2,4,3,0,1:T(8,128)(2,1)S(1)} %select_select_fusion), channel_id=1, replica_groups=mesh['grp'=32,'seq_0'=8,'seq_1'=2] {'seq_1'}, dimensions={1} | all-to-all | bytes 524288 | tf_op jit(solution)/shard_map/all_to_all | solution.py:48
  165.4 0.7 copy.84
  166.1 3.9 %all-to-all-start.1 = ((bf16[8,2,128,1,64]{2,4,3,1,0:T(8,128)(2,1)}), bf16[8,2,128,1,64]{2,4,3,1,0:T(8,128)(2,1)S(1)}, u32[]{:S(2)}, u32[]{:S(2)}) async-start(bf16[8,2,128,1,64]{2,4,3,1,0:T(8,128)(2,1)} %copy.84), calls=%async_computation.1 | async-start | bytes 524288 | tf_op jit(solution)/shard_map/all_to_all | solution.py:48
  170.0 6.2 %all-gather.11.cloned.1.call-done = bf16[16,64,512]{2,1,0:T(8,128)(2,1)} async-done(((bf16[1,64,512]{2,1,0:T(8,128)(2,1)}), bf16[16,64,512]{2,1,0:T(8,128)(2,1)}) %all-gather.11.cloned.1.call-update) | async-done | bytes 1048592 | tf_op jit(solution)/shard_map/all_gather | solution.py:151
  176.2 4.9 %all-to-all-done.1 = bf16[8,2,128,1,64]{2,4,3,1,0:T(8,128)(2,1)S(1)} async-done(((bf16[8,2,128,1,64]{2,4,3,1,0:T(8,128)(2,1)}), bf16[8,2,128,1,64]{2,4,3,1,0:T(8,128)(2,1)S(1)}, u32[]{:S(2)}, u32[]{:S(2)}) %all-to-all-start.1) | async-done | bytes 262176 | tf_op jit(solution)/shard_map/all_to_all | solution.py:48
  181.1 1.6 fusion.130
  182.7 1.2 fusion.20
  (73 shorter events, 10.3 us)
Async XLA Ops:
  6.5 1.6 copy-start
  6.5 77.8 %all-gather.7.cloned.1.call-start = ((), (), s32[]{:S(2)}) async-start(), calls=%async_computation.2 | async-start | bytes 4718592 | tf_op jit(solution)/shard_map/all_gather | solution.py:22
  8.2 2.8 %copy-start.4 = (f32[256,16]{0,1:T(8,128)S(1)}, f32[256,16]{0,1:T(8,128)}, u32[]{:S(2)}) copy-start(f32[256,16]{0,1:T(8,128)} %param.13) | copy-start | bytes 49156
  13.8 13.3 %copy-start.1 = (s32[1024]{0:T(1024)S(1)}, s32[1024]{0:T(1024)}, u32[]{:S(2)}) copy-start(s32[1024]{0:T(1024)} %param.12) | copy-start | bytes 12292
  27.0 107.0 %all-gather.9.cloned.1.call-start = ((), (), s32[]{:S(2)}) async-start(), calls=%async_computation.3 | async-start | bytes 2228224 | tf_op jit(solution)/shard_map/all_gather | solution.py:140
  88.9 1.0 copy-start.2
  88.9 1.3 copy-start.3
  88.9 1.3 copy-start.5
  89.3 2.0 %copy-start.6 = (f32[512]{0:T(512)S(1)}, f32[512]{0:T(512)}, u32[]{:S(2)}) copy-start(f32[512]{0:T(512)} %param.17) | copy-start | bytes 6148
  92.1 84.2 %all-gather.11.cloned.1.call-start = ((), (), s32[]{:S(2)}) async-start(), calls=%async_computation.4 | async-start | bytes 1114112 | tf_op jit(solution)/shard_map/all_gather | solution.py:151
  103.6 37.4 %copy-start.7 = (bf16[1,512,192]{1,2,0:T(8,128)(2,1)S(1)}, bf16[1,512,192]{1,2,0:T(8,128)(2,1)}, u32[]{:S(2)}) copy-start(bf16[1,512,192]{1,2,0:T(8,128)(2,1)} %param.18) | copy-start | bytes 589828
  166.1 15.0 %all-to-all-start.1 = ((bf16[8,2,128,1,64]{2,4,3,1,0:T(8,128)(2,1)}), bf16[8,2,128,1,64]{2,4,3,1,0:T(8,128)(2,1)S(1)}, u32[]{:S(2)}, u32[]{:S(2)}) async-start(bf16[8,2,128,1,64]{2,4,3,1,0:T(8,128)(2,1)} %copy.84), calls=%async_computation.1 | async-start | bytes 524288 | tf_op jit(solution)/shard_map/all_to_all | solution.py:48
Sparse Core Ops, SparseCore 0:
  27.1 57.1 all-gather.6
  92.2 41.7 all-gather.8
  136.1 40.1 all-gather.10
where the time goes:
time: 191 us; the launch traced here: 190 us
  waiting for transfers between devices  76.9 us (40%)
  blocking collectives  27.9 us (15%)
  matrix products  23.9 us (13%)
  local copies, waits for them, and re-layouts  23.1 us (12%)
  other arithmetic  17 us (9%)
  between operations  13.4 us (7%)
  loops' own time  4.2 us (2%)
  starting transfers between devices  3.96 us (2%)
    all_gather x1, waiting for transfers between devices, carried_in(): pieces = jax.tree.map(lambda part: lax.all_gather(part, axis), subtotal)  34.7 us
    all_gather x1, waiting for transfers between devices, shards(): gathered = lax.all_gather(rows_n, SEQ, axis=0, tiled=True)  30.4 us
    all_gather x3, blocking collectives, carried_in(): pieces = jax.tree.map(lambda part: lax.all_gather(part, axis), subtotal)  24.1 us
    and x1, other arithmetic, shards(): packed = jnp.take(gathered, index, axis=0)  10.1 us
    gather x1, local copies, waits for them, and re-layouts, shards(): packed = jnp.take(gathered, index, axis=0)  6.95 us
    gather x2, local copies, waits for them, and re-layouts, shards(): spread = jnp.take(outputs, jnp.clip(slot_group, 0, groups - 1), axis=0)  6.42 us
    all_gather x1, waiting for transfers between devices, shards(): full_out = lax.all_gather(attn_out, SEQ, axis=0, tiled=True)  6.25 us
    dot_general x1, matrix products, shards(): jnp.einsum('hij,jhp->ihp', decays * intersections[None], xs, precision=hi...  5.37 us
  transfers between devices with their start and end apart: 4, of which 4 were waited for; matrix products, arithmetic and copies ran while one was open for 23% of the time, Pallas kernels for 0%

commit v1 on v0

v1 whole, which is shorter than its diff:
```python
import jax
import jax.numpy as jnp
from jax import lax
from jax.experimental import pallas as pl
from jax.experimental.pallas import tpu as pltpu
from jax.sharding import PartitionSpec as P

MESH = pl.DeviceIdType.MESH
F32 = jnp.float32
BF16 = jnp.bfloat16

N = 16
RING = 8
TOK = 256
SUB = 128
D = 512
E = 1024
HEADS = 16
HDIM = 64
NST = 64
NG = 1024
MOST = 128
HALF = MOST // 2
QB = 256
BAND = QB + NG


def dot(a, b):
    return jnp.dot(a, b, preferred_element_type=F32)


def dot_nt(a, b):
    return lax.dot_general(a, b, (((1,), (1,)), ((), ())), preferred_element_type=F32)


def dot_tn(a, b):
    return lax.dot_general(a, b, (((0,), (0,)), ((), ())), preferred_element_type=F32)


def iota(shape, dim):
    return lax.broadcasted_iota(jnp.int32, shape, dim)


def two_terms(x):
    high = x.astype(BF16)
    return high, (x - high.astype(F32)).astype(BF16)


def spread(x, table):
    high, low = two_terms(x)
    return dot(high, table) + dot(low, table)


def layer(
    tokens,
    gpos,
    decay,
    w_in,
    gain,
    w_out,
    inner,
    w_qkv,
    w_back,
    out,
    total,
    pieces,
    arrived,
    states,
    state_in,
    proj,
    xs,
    inner_y,
    factor,
    hidden,
    place,
    rows,
    backs,
    qkv,
    packed,
    pick,
    outs,
    sent,
    heads,
    s_tot,
    r_tot,
    s_p,
    r_p,
    s_s,
    r_s,
    s_g,
    r_g,
    s_gs,
    r_gs,
    s_w,
    r_w,
    s_ws,
    r_ws,
    s_h,
    r_h,
):
    me = lax.axis_index("seq")
    chip = me // 2
    core = lax.rem(me, 2)
    sibling = chip * 2 + (1 - core)

    def on_ring(step):
        return lax.rem(chip + step + RING, RING) * 2 + core

    def remote(src, dst, s_sem, r_sem, to):
        return pltpu.make_async_remote_copy(
            src_ref=src,
            dst_ref=dst,
            send_sem=s_sem,
            recv_sem=r_sem,
            device_id={"seq": to},
            device_id_type=MESH,
        )

    def others(body):
        lax.fori_loop(1, N, lambda k, c: (body(lax.rem(me + k, N)), c)[1], 0)

    barrier = pltpu.get_barrier_semaphore()
    others(lambda d: pl.semaphore_signal(barrier, inc=1, device_id={"seq": d}, device_id_type=MESH))

    ld = decay[...]
    tri = (iota((TOK, TOK), 0) >= iota((TOK, TOK), 1)).astype(BF16)
    first, rest = two_terms(ld)
    second, third = two_terms(ld - first.astype(F32))
    cum = dot(tri, first) + dot(tri, second) + dot(tri, third)
    end = cum[TOK - 1 : TOK]
    total[me] = jnp.broadcast_to(jnp.pad(end, ((0, 0), (0, 128 - HEADS))), (8, 128))
    backs[me] = w_back[0]

    pl.semaphore_wait(barrier, N - 1)
    tot_copy = lambda d, src: remote(total.at[src], total.at[src], s_tot.at[d], r_tot.at[src], d)
    others(lambda d: tot_copy(d, me).start())

    def ring_send(buf, half, s_sem, r_sem, block, part, way, slot):
        ref = buf.at[block, pl.ds(part * half, half), :]
        return remote(ref, ref, s_sem.at[slot], r_sem.at[2 * block + part], on_ring(way))

    def ring_slot(step, part, way):
        return (step * 2 + part) * 2 + (way + 1) // 2

    def ring_step(buf, half, s_sem, r_sem, s_sib, r_sib, step):
        for part in range(2):
            for way in (1, -1):
                last = step == RING // 2
                if last and (part == 0) != (way == 1):
                    continue
                block = on_ring(-way * step)
                if step > 0:
                    ring_send(buf, half, s_sem, r_sem, block, part, way, 0).wait_recv()
                if step < RING // 2 - 1 or (step == RING // 2 - 1 and (part == 0) == (way == 1)):
                    ring_send(buf, half, s_sem, r_sem, block, part, way, ring_slot(step, part, way)).start()
        for way in (1, -1) if 0 < step < RING // 2 else (1,):
            block = on_ring(-way * step)
            remote(buf.at[block], buf.at[block], s_sib.at[block // 2], r_sib.at[block // 2], sibling).start()

    def ring_sibling_wait(buf, s_sib, r_sib, step):
        for way in (1, -1) if 0 < step < RING // 2 else (1,):
            block = on_ring(-way * step)
            other = (block // 2) * 2 + (1 - core)
            remote(buf.at[other], buf.at[other], s_sib.at[block // 2], r_sib.at[block // 2], sibling).wait_recv()

    def ring_done(buf, half, s_sem, r_sem, s_sib, r_sib):
        for step in range(RING // 2):
            for part in range(2):
                for way in (1, -1):
                    if step < RING // 2 - 1 or (part == 0) == (way == 1):
                        block = on_ring(-way * step)
                        ring_send(buf, half, s_sem, r_sem, block, part, way, ring_slot(step, part, way)).wait_send()
        for b in range(RING):
            block = b * 2 + core
            remote(buf.at[block], buf.at[block], s_sib.at[b], r_sib.at[b], sibling).wait_send()

    back_ring = (backs, HDIM // 2, s_w, r_w, s_ws, r_ws)
    row_ring = (rows, HALF, s_g, r_g, s_gs, r_gs)
    ring_step(*back_ring, 0)

    toks = tokens[...]
    for c in range(0, 2 * E + 2 * NST, 256):
        w = min(256, 2 * E + 2 * NST - c)
        proj[:, c : c + w] = dot(toks, w_in[:, c : c + w]).astype(BF16)

    mids = [cum[SUB // 2 - 1 : SUB // 2], cum[SUB + SUB // 2 - 1 : SUB + SUB // 2]]
    rel = jnp.concatenate([cum[:SUB] - mids[0], cum[SUB:] - mids[1]], axis=0)
    table = (iota((HEADS, E), 1) // HDIM == iota((HEADS, E), 0)).astype(BF16)
    f_in = spread(jnp.exp(rel), table)
    f_out = spread(jnp.exp(-rel), table)
    few = jnp.concatenate(
        [mids[0], mids[1], end - mids[0], end - mids[1], mids[1] - mids[0], end, end, end], axis=0
    )
    few = spread(jnp.exp(few), table)
    xs[...] = (proj[:, :E].astype(F32) * f_out).astype(BF16)
    bc = proj[:, 2 * E :]
    bmat, cmat = bc[:, :NST], bc[:, NST:]
    low = iota((SUB, SUB), 0) >= iota((SUB, SUB), 1)
    u = [dot_tn(bmat[k * SUB : (k + 1) * SUB], xs[k * SUB : (k + 1) * SUB]) for k in range(2)]
    local = (u[0] * few[2:3] + u[1] * few[3:4]).astype(BF16)
    for d in range(N):
        r, c = 16 * (d // 4), 256 * (d % 4)
        pieces[d] = local[r : r + 16, c : c + 256]

    p_copy = lambda d, src: remote(pieces.at[d], arrived.at[src], s_p.at[d], r_p.at[src], d)
    others(lambda d: p_copy(d, me).start())
    arrived[me] = pieces[me]

    u0 = (u[0] * few[4:5]).astype(BF16)
    for k in range(2):
        b_k, c_k = bmat[k * SUB : (k + 1) * SUB], cmat[k * SUB : (k + 1) * SUB]
        g = jnp.where(low, dot_nt(c_k, b_k), 0.0).astype(BF16)
        y = dot(g, xs[k * SUB : (k + 1) * SUB])
        if k == 1:
            y = y + dot(c_k, u0)
        inner_y[k * SUB : (k + 1) * SUB] = y
    gate = proj[:, E : 2 * E].astype(F32)
    factor[...] = f_in * (gate / (1.0 + jnp.exp(-gate)))

    others(lambda d: tot_copy(d, d).wait_recv())
    lanes = iota((128, 256), 1) // HDIM + 4 * lax.rem(me, 4)
    mine = (lanes == iota((128, 256), 0)).astype(BF16)
    sums = jnp.concatenate([total[d][0:1] for d in range(N)], axis=0)
    fades = spread(jnp.exp(sums), mine)

    others(lambda d: p_copy(d, d).wait_recv())
    run = jnp.zeros((16, 256), F32)
    for d in range(N):
        states[d] = run.astype(BF16)
        run = run * fades[d : d + 1] + arrived[d].astype(F32)
    s_copy = lambda d, src: remote(states.at[d], state_in.at[src], s_s.at[d], r_s.at[src], d)
    others(lambda d: s_copy(d, me).start())
    state_in[me] = states[me]

    ring_step(*back_ring, 1)

    gp = gpos[...]
    base = me * TOK
    before = [jnp.sum((gp < d * TOK).astype(jnp.int32)) for d in range(N)] + [jnp.int32(NG)]
    here = jnp.sum((gp < base).astype(jnp.int32))
    at = base + iota((TOK, 128), 0)
    less = jnp.zeros((TOK, 128), F32)
    same = jnp.zeros((TOK, 128), F32)
    for r in range(8):
        row = gp[r : r + 1]
        less = less + (row < at).astype(F32)
        same = same + (row == at).astype(F32)
    ones = jnp.ones((8, 128), BF16)
    rank = dot_nt(ones, less.astype(BF16))[0:1] - here.astype(F32)
    start = dot_nt(ones, same.astype(BF16))[0:1]
    place[...] = ((rank == iota((MOST, TOK), 0).astype(F32)) & (start > 0.5)).astype(BF16)

    others(lambda d: s_copy(d, d).wait_recv())
    ring_step(*back_ring, 2)

    squares = jnp.zeros((TOK, 1), F32)
    for q in range(4):
        cols = slice(256 * q, 256 * q + 256)
        s = jnp.concatenate([state_in[4 * k + q] for k in range(4)], axis=0).astype(F32)
        s = [(s * few[k : k + 1, cols]).astype(BF16) for k in range(2)]
        carried = jnp.concatenate([dot(cmat[k * SUB : (k + 1) * SUB], s[k]) for k in range(2)], axis=0)
        gated = (inner_y[:, cols] + carried) * factor[:, cols]
        inner_y[:, cols] = gated
        squares = squares + jnp.sum(gated * gated, axis=1, keepdims=True)
    scale = lax.rsqrt(squares * (1.0 / E) + 1e-5)
    normed = (inner_y[...] * scale * gain[...]).astype(BF16)
    hid = (toks.astype(F32) + dot(normed, w_out[...])).astype(BF16)
    hidden[...] = hid
    own = dot(place[...], hid)
    own = own * lax.rsqrt(jnp.mean(own * own, axis=1, keepdims=True) + 1e-5) * inner[...]
    rows[me] = own.astype(BF16)

    ring_step(*row_ring, 0)

    lane = iota((1, MOST), 1)
    slots = [jnp.where(lane + before[d] < before[d + 1], lane + before[d], -1) for d in range(N)]
    for p in range(NG // QB):
        for t in range(BAND // MOST):
            d = p * QB // MOST + t
            want = iota((QB, MOST), 0) + p * QB
            pick[p, :, t * MOST : (t + 1) * MOST] = (want == slots[d]).astype(BF16)
    outs[...] = jnp.zeros_like(outs)

    def project(block):
        qkv[pl.ds(pl.multiple_of(block * MOST, MOST), MOST), :] = dot(rows[block], w_qkv[0]).astype(BF16)

    project(me)
    for step in range(1, RING // 2 + 1):
        ring_step(*row_ring, step)
        if step == 1:
            ring_step(*back_ring, 3)
        if step == 2:
            ring_step(*back_ring, 4)
        ring_sibling_wait(rows, s_gs, r_gs, step - 1)
        for way in (1, -1) if 0 < step - 1 < RING // 2 else (1,):
            project((on_ring(-way * (step - 1)) // 2) * 2 + 1 - core)
        for way in (1, -1) if step < RING // 2 else (1,):
            project(on_ring(-way * step))
    ring_sibling_wait(rows, s_gs, r_gs, RING // 2)
    project((on_ring(RING // 2) // 2) * 2 + 1 - core)

    for p in range(NG // QB):
        packed[p * QB : (p + 1) * QB] = dot(pick[p], qkv[p * QB : p * QB + BAND]).astype(BF16)

    h_copy = lambda d, src: remote(sent.at[d], heads.at[src], s_h.at[d], r_h.at[src], d)

    def ship(d):
        block = outs[pl.ds(before[d], MOST), :]
        sent[d] = jnp.concatenate([block[:HALF], block[HALF:]], axis=1).astype(BF16)

        @pl.when(me != d)
        def _():
            h_copy(d, me).start()

    corner = iota((QB, QB), 0) >= iota((QB, QB), 1)
    shipped = 0
    for p in range(NG // QB):
        upto = (p + 1) * QB
        query = packed[p * QB : upto, :HDIM] * jnp.asarray(HDIM**-0.5, BF16)
        scores = dot_nt(query, packed[:upto, HDIM : 2 * HDIM])
        edge = jnp.where(corner, scores[:, p * QB :], -jnp.inf)
        scores = edge if p == 0 else jnp.concatenate([scores[:, : p * QB], edge], axis=1)
        expo = jnp.exp(scores - jnp.max(scores, axis=1, keepdims=True))
        weight = 1.0 / jnp.sum(expo, axis=1, keepdims=True)
        outs[p * QB : upto] = dot(expo.astype(BF16), packed[:upto, 2 * HDIM :]) * weight
        until = N if upto == NG else upto // MOST
        for d in range(shipped, until):
            ship(d)
        shipped = until
    heads[me] = sent[me]

    for step in range(RING // 2 + 1):
        ring_sibling_wait(backs, s_ws, r_ws, step)

    others(lambda d: h_copy(d, d).wait_recv())
    left = iota((HALF, 128), 1) < HDIM
    tops, bottoms = [], []
    for h in range(0, N, 2):
        a, b = heads[h].astype(F32), heads[h + 1].astype(F32)
        tops.append(jnp.where(left, a, pltpu.roll(b, HDIM, 1)).astype(BF16))
        bottoms.append(jnp.where(left, pltpu.roll(a, HDIM, 1), b).astype(BF16))
    joined = jnp.concatenate([jnp.concatenate(tops, axis=1), jnp.concatenate(bottoms, axis=1)], axis=0)
    back = dot(joined, backs[...].reshape(N * HDIM, D))
    high, lower = two_terms(back)
    put = place[...]
    out[...] = (hidden[...].astype(F32) + dot_tn(put, high) + dot_tn(put, lower)).astype(BF16)

    others(lambda d: tot_copy(d, me).wait_send())
    others(lambda d: p_copy(d, me).wait_send())
    others(lambda d: s_copy(d, me).wait_send())
    others(lambda d: h_copy(d, me).wait_send())
    ring_done(*back_ring)
    ring_done(*row_ring)


def shards(tokens, group_pos, log_decay, in_weight, norm_gain, out_weight, inner_gain, qkv_weight, attn_out):
    vmem = pl.BlockSpec(memory_space=pltpu.VMEM)
    dma = pltpu.SemaphoreType.DMA
    return pl.pallas_call(
        layer,
        out_shape=jax.ShapeDtypeStruct((TOK, D), BF16),
        in_specs=[vmem] * 9,
        out_specs=vmem,
        scratch_shapes=[
            pltpu.VMEM((N, 8, 128), F32),
            pltpu.VMEM((N, 16, 256), BF16),
            pltpu.VMEM((N, 16, 256), BF16),
            pltpu.VMEM((N, 16, 256), BF16),
            pltpu.VMEM((N, 16, 256), BF16),
            pltpu.VMEM((TOK, 2 * E + 2 * NST), BF16),
            pltpu.VMEM((TOK, E), BF16),
            pltpu.VMEM((TOK, E), F32),
            pltpu.VMEM((TOK, E), F32),
            pltpu.VMEM((TOK, D), BF16),
            pltpu.VMEM((MOST, TOK), BF16),
            pltpu.VMEM((N, MOST, D), BF16),
            pltpu.VMEM((N, HDIM, D), BF16),
            pltpu.VMEM((N * MOST, 3 * HDIM), BF16),
            pltpu.VMEM((NG, 3 * HDIM), BF16),
            pltpu.VMEM((NG // QB, QB, BAND), BF16),
            pltpu.VMEM((NG + MOST, HDIM), F32),
            pltpu.VMEM((N, HALF, 128), BF16),
            pltpu.VMEM((N, HALF, 128), BF16),
        ]
        + [dma((N,))] * 6
        + [dma((16,)), dma((2 * N,)), dma((RING,)), dma((RING,))] * 2
        + [dma((N,))] * 2,
        compiler_params=pltpu.CompilerParams(
            collective_id=0, has_side_effects=True, vmem_limit_bytes=48 * 2**20
        ),
    )(
        tokens,
        group_pos.reshape(8, NG // 8),
        log_decay,
        in_weight,
        norm_gain.reshape(1, E),
        out_weight,
        inner_gain.reshape(1, D),
        qkv_weight,
        attn_out,
    )


def solution(mesh):
    return jax.shard_map(
        shards,
        mesh=mesh,
        in_specs=(
            P(("grp", "seq"), None),
            P("grp"),
            P(("grp", "seq"), None),
            P(),
            P(),
            P(),
            P(),
            P("seq", None, None),
            P("seq", None, None),
        ),
        out_specs=P(("grp", "seq"), None),
        check_vma=False,
    )
```

time: 191 us -> 68.5 us (0.36)
  waiting for transfers between devices: 76.9 us -> 0 us
  Pallas kernels: 0 us -> 58.7 us
  blocking collectives: 27.9 us -> 0 us
  matrix products: 23.9 us -> 0 us
  other arithmetic: 17 us -> 0 us
  local copies, waits for them, and re-layouts: 23.1 us -> 9.27 us
  between operations: 13.4 us -> 0.03 us
  loops' own time: 4.2 us -> 0 us
  starting transfers between devices: 3.96 us -> 0 us
    all_gather x3 -> x0, waiting for transfers between devices: 71.3 us -> none  [the longest x1 34.7 us: carried_in(): pieces = jax.tree.map(lambda part: lax.all_gather(part, axis), subtotal)]
    pallas_call x0 -> x1, Pallas kernels: none -> 58.7 us  [shards(): pl.pallas_call(layer, out_shape=jax.ShapeDtypeStruct((TOK, D), BF16), in_...]
    all_gather x3 -> x0, blocking collectives: 24.1 us -> none  [carried_in(): pieces = jax.tree.map(lambda part: lax.all_gather(part, axis), subtotal)]
    dot_general x14 -> x0, matrix products: 23.9 us -> none  [the longest x1 5.37 us: shards(): jnp.einsum('hij,jhp->ihp', decays * intersections[None], xs, precision=hi...]
    gather x5 -> x0, local copies, waits for them, and re-layouts: 15.1 us -> none  [the longest x1 6.95 us: shards(): packed = jnp.take(gathered, index, axis=0)]
    and x2 -> x0, other arithmetic: 10.2 us -> none  [the longest x1 10.1 us: shards(): packed = jnp.take(gathered, index, axis=0)]
    unnamed x18 -> x17, local copies, waits for them, and re-layouts: 2.89 us -> 9.27 us
    all_to_all x1 -> x0, waiting for transfers between devices: 4.88 us -> none  [turned_blocks(): result = lax.all_to_all(result, axes[k], k, k, tiled=True)]
  transfers between devices with their start and end apart: 4 -> 0, of which waited for: 4 -> 0; matrix products, arithmetic and copies ran while one was open for 23% -> 0% of each run, Pallas kernels for 0% -> 0%
where the time goes in v1:
time: 68.5 us; the launch traced here: 68 us
  Pallas kernels  58.7 us (86%)
  local copies, waits for them, and re-layouts  9.27 us (14%)
    pallas_call x1, Pallas kernels, shards(): pl.pallas_call(layer, out_shape=jax.ShapeDtypeStruct((TOK, D), BF16), in_...  58.7 us
    unnamed x17, local copies, waits for them, and re-layouts  9.27 us

profile of v1, /device:TPU:1, one launch (start us, length us, event | category | flops | bytes accessed | tf_op | source)
XLA Modules:
  0.0 68.0 jit_solution(10369043103604710222)
XLA Ops:
  0.0 0.8 %copy.10.decay = f32[256,16]{1,0:T(8,128)S(1)} copy(f32[256,16]{0,1:T(8,128)} %param.11) | data formatting | bytes 32768 | tf_op args[2]
  0.8 1.1 %copy.11.w_qkv = bf16[1,512,192]{2,1,0:T(8,128)(2,1)S(1)} copy(bf16[1,512,192]{1,2,0:T(8,128)(2,1)} %param.16) | data formatting | bytes 393216 | tf_op args[7]
  1.9 0.0 copy-start
  1.9 1.6 %copy-done = bf16[512,2176]{1,0:T(8,128)(2,1)S(1)} copy-done((bf16[512,2176]{1,0:T(8,128)(2,1)S(1)}, bf16[512,2176]{1,0:T(8,128)(2,1)}, u32[]{:S(2)}) %copy-start) | copy-done | bytes 2228248
  3.5 0.0 copy-start.1
  3.5 1.2 %copy-done.1 = bf16[1024,512]{1,0:T(8,128)(2,1)S(1)} copy-done((bf16[1024,512]{1,0:T(8,128)(2,1)S(1)}, bf16[1024,512]{1,0:T(8,128)(2,1)}, u32[]{:S(2)}) %copy-start.1) | copy-done | bytes 1048600
  4.7 0.0 copy-start.2
  4.7 0.9 %copy-done.2 = bf16[256,512]{1,0:T(8,128)(2,1)S(1)} copy-done((bf16[256,512]{1,0:T(8,128)(2,1)S(1)}, bf16[256,512]{1,0:T(8,128)(2,1)}, u32[]{:S(2)}) %copy-start.2) | copy-done | bytes 262168
  5.7 0.0 copy-start.3
  5.7 0.8 %copy-done.3 = bf16[1,64,512]{2,1,0:T(8,128)(2,1)S(1)} copy-done((bf16[1,64,512]{2,1,0:T(8,128)(2,1)S(1)}, bf16[1,64,512]{2,1,0:T(8,128)(2,1)}, u32[]{:S(2)}) %copy-start.3) | copy-done | bytes 65560
  6.5 0.0 copy-start.4
  6.5 0.7 %copy-done.4 = s32[1024]{0:T(1024)S(1)} copy-done((s32[1024]{0:T(1024)S(1)}, s32[1024]{0:T(1024)}, u32[]{:S(2)}) %copy-start.4) | copy-done | bytes 4120
  7.2 0.0 copy-start.5
  7.2 0.7 %copy-done.5 = f32[1024]{0:T(1024)S(1)} copy-done((f32[1024]{0:T(1024)S(1)}, f32[1024]{0:T(1024)}, u32[]{:S(2)}) %copy-start.5) | copy-done | bytes 4120
  7.9 0.0 copy-start.6
  7.9 0.7 copy-done.6
  8.6 58.7 %shard_map.91 = bf16[256,512]{1,0:T(8,128)(2,1)S(1)} custom-call(bf16[256,512]{1,0:T(8,128)(2,1)S(1)} %copy-done.2, s32[8,128]{1,0:T(8,128)S(1)} %bitcast.3, f32[256,16]{1,0:T(8,128)S(1)} %copy.10.decay, bf16[512,2176]{1,0:T(8,128)(2,1)S(1)} %copy-done, f32[1,1024]{1,0:T(1,128)S(1)} %bitcast.4, bf16[1024,512]{1,0:T(8,128)(2,1)S(1)} %copy-done.1, ...), custom_call_target="tpu_custom_call" | custom-call | tf_op jit(solution)/shard_map/pallas_call | solution.py:359
  67.3 0.7 %copy.13 = bf16[256,512]{1,0:T(8,128)(2,1)} copy(bf16[256,512]{1,0:T(8,128)(2,1)S(1)} %shard_map.91) | data formatting | bytes 524288
Async XLA Ops:
  1.9 1.6 %copy-start = (bf16[512,2176]{1,0:T(8,128)(2,1)S(1)}, bf16[512,2176]{1,0:T(8,128)(2,1)}, u32[]{:S(2)}) copy-start(bf16[512,2176]{1,0:T(8,128)(2,1)} %w_in.1) | copy-start | bytes 6684676
  3.5 1.2 %copy-start.1 = (bf16[1024,512]{1,0:T(8,128)(2,1)S(1)}, bf16[1024,512]{1,0:T(8,128)(2,1)}, u32[]{:S(2)}) copy-start(bf16[1024,512]{1,0:T(8,128)(2,1)} %w_out.1) | copy-start | bytes 3145732
  4.7 0.9 %copy-start.2 = (bf16[256,512]{1,0:T(8,128)(2,1)S(1)}, bf16[256,512]{1,0:T(8,128)(2,1)}, u32[]{:S(2)}) copy-start(bf16[256,512]{1,0:T(8,128)(2,1)} %tokens.1) | copy-start | bytes 786436
  5.7 0.8 %copy-start.3 = (bf16[1,64,512]{2,1,0:T(8,128)(2,1)S(1)}, bf16[1,64,512]{2,1,0:T(8,128)(2,1)}, u32[]{:S(2)}) copy-start(bf16[1,64,512]{2,1,0:T(8,128)(2,1)} %w_back.1) | copy-start | bytes 196612
  6.5 0.7 %copy-start.4 = (s32[1024]{0:T(1024)S(1)}, s32[1024]{0:T(1024)}, u32[]{:S(2)}) copy-start(s32[1024]{0:T(1024)} %param.10) | copy-start | bytes 12292
  7.2 0.7 %copy-start.5 = (f32[1024]{0:T(1024)S(1)}, f32[1024]{0:T(1024)}, u32[]{:S(2)}) copy-start(f32[1024]{0:T(1024)} %param.13) | copy-start | bytes 12292
  7.9 0.7 %copy-start.6 = (f32[512]{0:T(512)S(1)}, f32[512]{0:T(512)}, u32[]{:S(2)}) copy-start(f32[512]{0:T(512)} %param.15) | copy-start | bytes 6148

commit v2 on v1

v2 whole, which is shorter than its diff:
```python
import functools

import jax
import jax.numpy as jnp
from jax import lax
from jax.experimental import pallas as pl
from jax.experimental.pallas import tpu as pltpu
from jax.sharding import PartitionSpec as P

MESH = pl.DeviceIdType.MESH
F32 = jnp.float32
BF16 = jnp.bfloat16

N = 16
RING = 8
TOK = 256
SUB = 128
D = 512
E = 1024
HEADS = 16
HDIM = 64
NST = 64
NG = 1024
MOST = 128
HALF = MOST // 2
W_IN = 2 * E + 2 * NST
PARTS = 4
QB = 256
BAND = QB + NG


FAR_FIRST = sorted(range(1, N), key=lambda k: -min(k, N - k))


def dot(a, b):
    return jnp.dot(a, b, preferred_element_type=F32)


def dot_nt(a, b):
    return lax.dot_general(a, b, (((1,), (1,)), ((), ())), preferred_element_type=F32)


def dot_tn(a, b):
    return lax.dot_general(a, b, (((0,), (0,)), ((), ())), preferred_element_type=F32)


def iota(shape, dim):
    return lax.broadcasted_iota(jnp.int32, shape, dim)


def two_terms(x):
    high = x.astype(BF16)
    return high, (x - high.astype(F32)).astype(BF16)


def spread(x, table):
    high, low = two_terms(x)
    return dot(high, table) + dot(low, table)


def layer(
    tokens_h,
    gpos_h,
    decay_h,
    w_in_h,
    gain_h,
    w_out_h,
    inner_h,
    w_qkv_h,
    w_back_h,
    out,
    tokens,
    gpos,
    decay,
    w_in,
    gain,
    w_out,
    inner,
    w_qkv,
    total,
    pieces,
    arrived,
    states,
    state_in,
    proj,
    xs,
    inner_y,
    factor,
    hidden,
    place,
    rows,
    backs,
    qkv,
    packed,
    pick,
    outs,
    firsts,
    sent,
    heads,
    loaded,
    s_tot,
    r_tot,
    s_p,
    r_p,
    s_s,
    r_s,
    s_g,
    r_g,
    s_gs,
    r_gs,
    s_w,
    r_w,
    s_ws,
    r_ws,
    s_h,
    r_h,
):
    me = lax.axis_index("seq")
    chip = me // 2
    core = lax.rem(me, 2)
    sibling = chip * 2 + (1 - core)

    def on_ring(step):
        return lax.rem(chip + step + RING, RING) * 2 + core

    def remote(src, dst, s_sem, r_sem, to):
        return pltpu.make_async_remote_copy(
            src_ref=src,
            dst_ref=dst,
            send_sem=s_sem,
            recv_sem=r_sem,
            device_id={"seq": to},
            device_id_type=MESH,
        )

    def others(body):
        for k in FAR_FIRST:
            body(lax.rem(me + k, N))

    wide = [pl.ds(0, E), pl.ds(2 * E, 2 * NST), pl.ds(E, E)]
    load = {
        name: pltpu.make_async_copy(src, dst, loaded.at[k])
        for k, (name, src, dst) in enumerate(
            (
                ("decay", decay_h, decay),
                ("tokens", tokens_h, tokens),
                *((c, w_in_h.at[:, cols], w_in.at[:, cols]) for c, cols in enumerate(wide)),
                ("back", w_back_h.at[0], backs.at[me]),
                ("gpos", gpos_h, gpos),
                ("gain", gain_h, gain),
                ("out", w_out_h, w_out),
                ("inner", inner_h, inner),
                ("qkv", w_qkv_h.at[0], w_qkv),
            )
        )
    }
    late = (2, "gpos", "gain", "out", "inner", "qkv")
    for name, copy in load.items():
        if name not in late:
            copy.start()
    barrier = pltpu.get_barrier_semaphore()
    others(lambda d: pl.semaphore_signal(barrier, inc=1, device_id={"seq": d}, device_id_type=MESH))

    load["decay"].wait()
    ld = decay[...]
    tri = (iota((TOK, TOK), 0) >= iota((TOK, TOK), 1)).astype(BF16)
    first, rest = two_terms(ld)
    second, third = two_terms(ld - first.astype(F32))
    cum = dot_nt(tri, first) + dot_nt(tri, second) + dot_nt(tri, third)
    end = cum[TOK - 1 : TOK]
    total[me] = jnp.pad(end, ((0, 0), (0, 128 - HEADS)))

    pl.semaphore_wait(barrier, N - 1)
    tot_copy = lambda d, src: remote(total.at[src], total.at[src], s_tot.at[d], r_tot.at[src], d)
    others(lambda d: tot_copy(d, me).start())

    def ring_copy(ring, block, part, way, hops, slot):
        buf, parts, s_sem, r_sem, _, _ = ring
        size = buf.shape[1] // parts
        ref = buf.at[block, pl.ds(part * size, size), :]
        return remote(ref, ref, s_sem.at[slot], r_sem.at[parts * block + part], on_ring(hops * way))

    def ring_near(parts, part, way):
        return (part < parts // 2) == (way == 1)

    def ring_sends(ring, step):
        parts = ring[1]
        for part in range(parts):
            for way in (1, -1):
                slot = (step * parts + part) * 2 + (way + 1) // 2
                yield part, way, ring_copy(ring, on_ring(-way * step), part, way, 1, slot)
        for part in range(parts) if step == 2 else ():
            for way in (1, -1):
                if ring_near(parts, part, way):
                    slot = (3 * parts + part) * 2 + (way + 1) // 2
                    yield None, way, ring_copy(ring, on_ring(-way * step), part, way, 2, slot)

    def ring_wait(ring, step, part, way):
        ring_copy(ring, on_ring(-way * step), part, way, 1, 0).wait_recv()

    def ring_hand(ring, block):
        buf, _, _, _, s_sib, r_sib = ring
        return remote(buf.at[block], buf.at[block], s_sib.at[block // 2], r_sib.at[block // 2], sibling)

    def ring_ways(step):
        return (1, -1) if 0 < step < RING // 2 else (1,)

    def ring_step(ring, step):
        parts = ring[1]
        if step <= 2:
            for part, way, copy in ring_sends(ring, step):
                if step > 0 and part is not None:
                    ring_wait(ring, step, part, way)
                copy.start()
        else:
            for part in range(parts):
                for way in (1, -1):
                    if step == 3 or ring_near(parts, part, way):
                        ring_wait(ring, step, part, way)
        for way in ring_ways(step):
            ring_hand(ring, on_ring(-way * step)).start()

    def ring_sibling_wait(ring, step):
        for way in ring_ways(step):
            ring_hand(ring, (on_ring(-way * step) // 2) * 2 + 1 - core).wait_recv()

    def ring_done(ring):
        for step in range(3):
            for _, _, copy in ring_sends(ring, step):
                copy.wait_send()
        for b in range(RING):
            ring_hand(ring, b * 2 + core).wait_send()

    back_ring = (backs, 2, s_w, r_w, s_ws, r_ws)
    row_ring = (rows, PARTS, s_g, r_g, s_gs, r_gs)
    load["back"].wait()
    ring_step(back_ring, 0)

    load["tokens"].wait()
    toks = tokens[...]

    def project_in(c):
        load[c].wait()
        proj[:, wide[c]] = dot(toks, w_in[:, wide[c]]).astype(BF16)

    project_in(0)
    project_in(1)
    for name in late:
        load[name].start()

    mids = [cum[SUB // 2 - 1 : SUB // 2], cum[SUB + SUB // 2 - 1 : SUB + SUB // 2]]
    rel = jnp.concatenate([cum[:SUB] - mids[0], cum[SUB:] - mids[1]], axis=0)
    table = (iota((HEADS, E), 1) // HDIM == iota((HEADS, E), 0)).astype(BF16)
    f_in = spread(jnp.exp(rel), table)
    f_out = spread(jnp.exp(-rel), table)
    few = jnp.concatenate(
        [mids[0], mids[1], end - mids[0], end - mids[1], mids[1] - mids[0], end, end, end], axis=0
    )
    few = spread(jnp.exp(few), table)
    xs[...] = (proj[:, :E].astype(F32) * f_out).astype(BF16)
    bc = proj[:, 2 * E :]
    bmat, cmat = bc[:, :NST], bc[:, NST:]
    low = iota((SUB, SUB), 0) >= iota((SUB, SUB), 1)
    u = [dot_tn(bmat[k * SUB : (k + 1) * SUB], xs[k * SUB : (k + 1) * SUB]) for k in range(2)]
    local = (u[0] * few[2:3] + u[1] * few[3:4]).astype(BF16)
    for d in range(N):
        r, c = 16 * (d // 4), 256 * (d % 4)
        pieces[d] = local[r : r + 16, c : c + 256]

    p_copy = lambda d, src: remote(pieces.at[d], arrived.at[src], s_p.at[d], r_p.at[src], d)
    others(lambda d: p_copy(d, me).start())
    arrived[me] = pieces[me]

    load["gpos"].wait()
    gp = gpos[...]
    base = me * TOK
    before = [jnp.sum((gp < d * TOK).astype(jnp.int32)) for d in range(N)] + [jnp.int32(NG)]
    for d in range(N):
        firsts[d] = before[d]
    here = firsts[me]
    at = base + iota((TOK, 128), 0)
    less = jnp.zeros((TOK, 128), F32)
    same = jnp.zeros((TOK, 128), F32)
    for r in range(8):
        row = gp[r : r + 1]
        less = less + (row < at).astype(F32)
        same = same + (row == at).astype(F32)
    ones = jnp.ones((8, 128), BF16)
    rank = dot_nt(ones, less.astype(BF16))[0:1] - here.astype(F32)
    start = dot_nt(ones, same.astype(BF16))[0:1]
    place[...] = ((rank == iota((MOST, TOK), 0).astype(F32)) & (start > 0.5)).astype(BF16)

    u0 = (u[0] * few[4:5]).astype(BF16)
    for k in range(2):
        b_k, c_k = bmat[k * SUB : (k + 1) * SUB], cmat[k * SUB : (k + 1) * SUB]
        g = jnp.where(low, dot_nt(c_k, b_k), 0.0).astype(BF16)
        y = dot(g, xs[k * SUB : (k + 1) * SUB])
        if k == 1:
            y = y + dot(c_k, u0)
        inner_y[k * SUB : (k + 1) * SUB] = y
    project_in(2)
    gate = proj[:, E : 2 * E].astype(F32)
    factor[...] = f_in * (gate / (1.0 + jnp.exp(-gate)))

    others(lambda d: tot_copy(d, d).wait_recv())
    lanes = iota((128, 256), 1) // HDIM + 4 * lax.rem(me, 4)
    mine = (lanes == iota((128, 256), 0)).astype(BF16)
    sums = jnp.concatenate([total[d] for d in range(N)], axis=0)
    fades = spread(jnp.exp(sums), mine)

    others(lambda d: p_copy(d, d).wait_recv())
    run = jnp.zeros((16, 256), F32)
    for d in range(N):
        states[d] = run.astype(BF16)
        run = run * fades[d : d + 1] + arrived[d].astype(F32)
    s_copy = lambda d, src: remote(states.at[d], state_in.at[src], s_s.at[d], r_s.at[src], d)
    others(lambda d: s_copy(d, me).start())
    state_in[me] = states[me]

    others(lambda d: s_copy(d, d).wait_recv())
    ring_step(back_ring, 1)

    squares = jnp.zeros((TOK, 1), F32)
    for q in range(4):
        cols = slice(256 * q, 256 * q + 256)
        s = jnp.concatenate([state_in[4 * k + q] for k in range(4)], axis=0).astype(F32)
        s = [(s * few[k : k + 1, cols]).astype(BF16) for k in range(2)]
        carried = jnp.concatenate([dot(cmat[k * SUB : (k + 1) * SUB], s[k]) for k in range(2)], axis=0)
        gated = (inner_y[:, cols] + carried) * factor[:, cols]
        inner_y[:, cols] = gated
        squares = squares + jnp.sum(gated * gated, axis=1, keepdims=True)
    for name in ("gain", "out", "inner", "qkv"):
        load[name].wait()
    scale = lax.rsqrt(squares * (1.0 / E) + 1e-5)
    normed = (inner_y[...] * scale * gain[...]).astype(BF16)
    hid = (toks.astype(F32) + dot(normed, w_out[...])).astype(BF16)
    hidden[...] = hid
    own = dot(place[...], hid)
    own = own * lax.rsqrt(jnp.mean(own * own, axis=1, keepdims=True) + 1e-5) * inner[...]
    rows[me] = own.astype(BF16)

    ring_step(row_ring, 0)

    lane = iota((1, MOST), 1)
    slots = [jnp.where(lane + before[d] < before[d + 1], lane + before[d], -1) for d in range(N)]
    for p in range(NG // QB):
        for t in range(BAND // MOST):
            d = p * QB // MOST + t
            want = iota((QB, MOST), 0) + p * QB
            pick[p, :, t * MOST : (t + 1) * MOST] = (want == slots[d]).astype(BF16)
    outs[...] = jnp.zeros_like(outs)

    def project(block):
        qkv[pl.ds(pl.multiple_of(block * MOST, MOST), MOST), :] = dot_nt(rows[block], w_qkv[...]).astype(BF16)

    project(me)
    for step in range(1, RING // 2 + 1):
        ring_step(row_ring, step)
        ring_sibling_wait(row_ring, step - 1)
        for way in ring_ways(step - 1):
            project((on_ring(-way * (step - 1)) // 2) * 2 + 1 - core)
        for way in ring_ways(step):
            project(on_ring(-way * step))
    ring_sibling_wait(row_ring, RING // 2)
    project((on_ring(RING // 2) // 2) * 2 + 1 - core)
    ring_step(back_ring, 2)

    for p in range(NG // QB):
        packed[p * QB : (p + 1) * QB] = dot(pick[p], qkv[p * QB : p * QB + BAND]).astype(BF16)

    h_copy = lambda d, src: remote(sent.at[d], heads.at[src], s_h.at[d], r_h.at[src], d)

    def pack_head(d):
        block = outs[pl.ds(firsts[d], MOST), :]
        return jnp.concatenate([block[:HALF], block[HALF:]], axis=1).astype(BF16)

    def ship(d):
        sent[d] = pack_head(d)
        h_copy(d, me).start()

    corner = iota((QB, QB), 0) >= iota((QB, QB), 1)
    shipped = 0
    for p in range(NG // QB):
        upto = (p + 1) * QB
        query = packed[p * QB : upto, :HDIM] * jnp.asarray(HDIM**-0.5, BF16)
        scores = dot_nt(query, packed[:upto, HDIM : 2 * HDIM])
        edge = jnp.where(corner, scores[:, p * QB :], -jnp.inf)
        scores = edge if p == 0 else jnp.concatenate([scores[:, : p * QB], edge], axis=1)
        expo = jnp.exp(scores - jnp.max(scores, axis=1, keepdims=True))
        weight = 1.0 / jnp.sum(expo, axis=1, keepdims=True)
        outs[p * QB : upto] = dot(expo.astype(BF16), packed[:upto, 2 * HDIM :]) * weight
        if upto < NG:
            for d in range(shipped, upto // MOST):
                pl.when(me != d)(functools.partial(ship, d))
            shipped = upto // MOST
    for k in FAR_FIRST:
        d = lax.rem(me + k, N)
        pl.when(d >= shipped)(functools.partial(ship, d))
    heads[me] = pack_head(me)

    for step in (3, 4):
        ring_step(back_ring, step)
    for step in range(RING // 2 + 1):
        ring_sibling_wait(back_ring, step)

    others(lambda d: h_copy(d, d).wait_recv())
    left = iota((HALF, 128), 1) < HDIM
    tops, bottoms = [], []
    for h in range(0, N, 2):
        a, b = heads[h].astype(F32), heads[h + 1].astype(F32)
        tops.append(jnp.where(left, a, pltpu.roll(b, HDIM, 1)).astype(BF16))
        bottoms.append(jnp.where(left, pltpu.roll(a, HDIM, 1), b).astype(BF16))
    joined = jnp.concatenate([jnp.concatenate(tops, axis=1), jnp.concatenate(bottoms, axis=1)], axis=0)
    back = dot(joined, backs[...].reshape(N * HDIM, D))
    high, lower = two_terms(back)
    put = place[...]
    out[...] = (hidden[...].astype(F32) + dot_tn(put, high) + dot_tn(put, lower)).astype(BF16)

    others(lambda d: tot_copy(d, me).wait_send())
    others(lambda d: p_copy(d, me).wait_send())
    others(lambda d: s_copy(d, me).wait_send())
    others(lambda d: h_copy(d, me).wait_send())
    ring_done(back_ring)
    ring_done(row_ring)


def shards(tokens, group_pos, log_decay, in_weight, norm_gain, out_weight, inner_gain, qkv_weight, attn_out):
    vmem = pl.BlockSpec(memory_space=pltpu.VMEM)
    hbm = pl.BlockSpec(memory_space=pltpu.HBM)
    dma = pltpu.SemaphoreType.DMA
    return pl.pallas_call(
        layer,
        out_shape=jax.ShapeDtypeStruct((TOK, D), BF16),
        in_specs=[hbm] * 9,
        out_specs=vmem,
        scratch_shapes=[
            pltpu.VMEM((TOK, D), BF16),
            pltpu.VMEM((8, NG // 8), jnp.int32),
            pltpu.VMEM((HEADS, TOK), F32),
            pltpu.VMEM((D, W_IN), BF16),
            pltpu.VMEM((1, E), F32),
            pltpu.VMEM((E, D), BF16),
            pltpu.VMEM((1, D), F32),
            pltpu.VMEM((3 * HDIM, D), BF16),
            pltpu.VMEM((N, 1, 128), F32),
            pltpu.VMEM((N, 16, 256), BF16),
            pltpu.VMEM((N, 16, 256), BF16),
            pltpu.VMEM((N, 16, 256), BF16),
            pltpu.VMEM((N, 16, 256), BF16),
            pltpu.VMEM((TOK, W_IN), BF16),
            pltpu.VMEM((TOK, E), BF16),
            pltpu.VMEM((TOK, E), F32),
            pltpu.VMEM((TOK, E), F32),
            pltpu.VMEM((TOK, D), BF16),
            pltpu.VMEM((MOST, TOK), BF16),
            pltpu.VMEM((N, MOST, D), BF16),
            pltpu.VMEM((N, HDIM, D), BF16),
            pltpu.VMEM((N * MOST, 3 * HDIM), BF16),
            pltpu.VMEM((NG, 3 * HDIM), BF16),
            pltpu.VMEM((NG // QB, QB, BAND), BF16),
            pltpu.VMEM((NG + MOST, HDIM), F32),
            pltpu.SMEM((N,), jnp.int32),
            pltpu.VMEM((N, HALF, 128), BF16),
            pltpu.VMEM((N, HALF, 128), BF16),
        ]
        + [dma((11,))]
        + [dma((N,))] * 6
        + [dma((RING * PARTS,)), dma((N * PARTS,)), dma((RING,)), dma((RING,))] * 2
        + [dma((N,))] * 2,
        compiler_params=pltpu.CompilerParams(
            collective_id=0, has_side_effects=True, vmem_limit_bytes=60 * 2**20
        ),
    )(
        tokens,
        group_pos.reshape(8, NG // 8),
        log_decay.T,
        in_weight,
        norm_gain.reshape(1, E),
        out_weight,
        inner_gain.reshape(1, D),
        qkv_weight.transpose(0, 2, 1),
        attn_out,
    )


def solution(mesh):
    return jax.shard_map(
        shards,
        mesh=mesh,
        in_specs=(
            P(("grp", "seq"), None),
            P("grp"),
            P(("grp", "seq"), None),
            P(),
            P(),
            P(),
            P(),
            P("seq", None, None),
            P("seq", None, None),
        ),
        out_specs=P(("grp", "seq"), None),
        check_vma=False,
    )
```

time: 68.5 us -> 58.2 us (0.85)
  local copies, waits for them, and re-layouts: 9.27 us -> 1.67 us
  Pallas kernels: 58.7 us -> 56.4 us
    unnamed x17 -> x1, local copies, waits for them, and re-layouts: 9.27 us -> 1.67 us
    pallas_call x1, Pallas kernels: 58.7 us -> 56.4 us  [shards(): pl.pallas_call(layer, out_shape=jax.ShapeDtypeStruct((TOK, D), BF16), in_...]
where the time goes in v2:
time: 58.2 us; the launch traced here: 58 us
  Pallas kernels  56.4 us (97%)
  local copies, waits for them, and re-layouts  1.67 us (3%)
    pallas_call x1, Pallas kernels, shards(): pl.pallas_call(layer, out_shape=jax.ShapeDtypeStruct((TOK, D), BF16), in_...  56.4 us
    unnamed x1, local copies, waits for them, and re-layouts  1.67 us

profile of v2, /device:TPU:1, one launch (start us, length us, event | category | flops | bytes accessed | tf_op | source)
XLA Modules:
  0.0 58.0 jit_solution(4075318451208541651)
XLA Ops:
  0.0 56.4 %shard_map.91 = bf16[256,512]{1,0:T(8,128)(2,1)} custom-call(bf16[256,512]{1,0:T(8,128)(2,1)} %tokens_h.1, s32[8,128]{1,0:T(8,128)} %bitcast.7, f32[16,256]{1,0:T(8,128)} %bitcast.6, bf16[512,2176]{1,0:T(8,128)(2,1)} %w_in_h.1, f32[1,1024]{1,0:T(1,128)} %bitcast.8, bf16[1024,512]{1,0:T(8,128)(2,1)} %w_out_h.1, f32[1,512]{1,0:T(1,128)} %bitcast.9, ...), custom_call_target="tpu_custom_call" | custom-call | tf_op jit(solution)/shard_map/pallas_call | solution.py:431
  56.4 1.7 %copy.11 = bf16[256,512]{1,0:T(8,128)(2,1)} copy(bf16[256,512]{1,0:T(8,128)(2,1)} %shard_map.91) | data formatting | bytes 524288

commit v3 on v2

--- a/solution.py
+++ b/solution.py
@@ -25,7 +25,7 @@
 HALF = MOST // 2
 W_IN = 2 * E + 2 * NST
 PARTS = 4
-QB = 256
+QB = 512
 BAND = QB + NG
 
 
@@ -88,6 +88,7 @@
     factor,
     hidden,
     place,
+    put,
     rows,
     backs,
     qkv,
@@ -170,9 +171,7 @@
     end = cum[TOK - 1 : TOK]
     total[me] = jnp.pad(end, ((0, 0), (0, 128 - HEADS)))
 
-    pl.semaphore_wait(barrier, N - 1)
     tot_copy = lambda d, src: remote(total.at[src], total.at[src], s_tot.at[d], r_tot.at[src], d)
-    others(lambda d: tot_copy(d, me).start())
 
     def ring_copy(ring, block, part, way, hops, slot):
         buf, parts, s_sem, r_sem, _, _ = ring
@@ -187,13 +186,12 @@
         parts = ring[1]
         for part in range(parts):
             for way in (1, -1):
-                slot = (step * parts + part) * 2 + (way + 1) // 2
-                yield part, way, ring_copy(ring, on_ring(-way * step), part, way, 1, slot)
-        for part in range(parts) if step == 2 else ():
-            for way in (1, -1):
-                if ring_near(parts, part, way):
-                    slot = (3 * parts + part) * 2 + (way + 1) // 2
-                    yield None, way, ring_copy(ring, on_ring(-way * step), part, way, 2, slot)
+                block = on_ring(-way * step)
+                slot = part * 2 + (way + 1) // 2
+                copies = [ring_copy(ring, block, part, way, 1, 2 * parts * step + slot)]
+                if step == 2 and ring_near(parts, part, way):
+                    copies.insert(0, ring_copy(ring, block, part, way, 2, 6 * parts + slot))
+                yield part, way, copies
 
     def ring_wait(ring, step, part, way):
         ring_copy(ring, on_ring(-way * step), part, way, 1, 0).wait_recv()
@@ -208,10 +206,11 @@
     def ring_step(ring, step):
         parts = ring[1]
         if step <= 2:
-            for part, way, copy in ring_sends(ring, step):
-                if step > 0 and part is not None:
+            for part, way, copies in ring_sends(ring, step):
+                if step > 0:
                     ring_wait(ring, step, part, way)
-                copy.start()
+                for copy in copies:
+                    copy.start()
         else:
             for part in range(parts):
                 for way in (1, -1):
@@ -226,15 +225,14 @@
 
     def ring_done(ring):
         for step in range(3):
-            for _, _, copy in ring_sends(ring, step):
-                copy.wait_send()
+            for _, _, copies in ring_sends(ring, step):
+                for copy in copies:
+                    copy.wait_send()
         for b in range(RING):
             ring_hand(ring, b * 2 + core).wait_send()
 
     back_ring = (backs, 2, s_w, r_w, s_ws, r_ws)
     row_ring = (rows, PARTS, s_g, r_g, s_gs, r_gs)
-    load["back"].wait()
-    ring_step(back_ring, 0)
 
     load["tokens"].wait()
     toks = tokens[...]
@@ -268,7 +266,11 @@
         pieces[d] = local[r : r + 16, c : c + 256]
 
     p_copy = lambda d, src: remote(pieces.at[d], arrived.at[src], s_p.at[d], r_p.at[src], d)
+    pl.semaphore_wait(barrier, N - 1)
+    others(lambda d: tot_copy(d, me).start())
     others(lambda d: p_copy(d, me).start())
+    load["back"].wait()
+    ring_step(back_ring, 0)
     arrived[me] = pieces[me]
 
     load["gpos"].wait()
@@ -288,7 +290,10 @@
     ones = jnp.ones((8, 128), BF16)
     rank = dot_nt(ones, less.astype(BF16))[0:1] - here.astype(F32)
     start = dot_nt(ones, same.astype(BF16))[0:1]
-    place[...] = ((rank == iota((MOST, TOK), 0).astype(F32)) & (start > 0.5)).astype(BF16)
+    one_hot = jnp.where((rank == iota((MOST, TOK), 0).astype(F32)) & (start > 0.5), 1.0, 0.0)
+    place[...] = one_hot.astype(BF16)
+    back_to = one_hot.T.astype(BF16)
+    put[...] = jnp.concatenate([back_to, back_to], axis=1)
 
     u0 = (u[0] * few[4:5]).astype(BF16)
     for k in range(2):
@@ -412,9 +417,8 @@
         bottoms.append(jnp.where(left, pltpu.roll(a, HDIM, 1), b).astype(BF16))
     joined = jnp.concatenate([jnp.concatenate(tops, axis=1), jnp.concatenate(bottoms, axis=1)], axis=0)
     back = dot(joined, backs[...].reshape(N * HDIM, D))
-    high, lower = two_terms(back)
-    put = place[...]
-    out[...] = (hidden[...].astype(F32) + dot_tn(put, high) + dot_tn(put, lower)).astype(BF16)
+    placed = dot(put[...], jnp.concatenate(two_terms(back), axis=0))
+    out[...] = (hidden[...].astype(F32) + placed).astype(BF16)
 
     others(lambda d: tot_copy(d, me).wait_send())
     others(lambda d: p_copy(d, me).wait_send())
@@ -453,6 +457,7 @@
             pltpu.VMEM((TOK, E), F32),
             pltpu.VMEM((TOK, D), BF16),
             pltpu.VMEM((MOST, TOK), BF16),
+            pltpu.VMEM((TOK, 2 * MOST), BF16),
             pltpu.VMEM((N, MOST, D), BF16),
             pltpu.VMEM((N, HDIM, D), BF16),
             pltpu.VMEM((N * MOST, 3 * HDIM), BF16),
@@ -468,18 +473,23 @@
         + [dma((RING * PARTS,)), dma((N * PARTS,)), dma((RING,)), dma((RING,))] * 2
         + [dma((N,))] * 2,
         compiler_params=pltpu.CompilerParams(
-            collective_id=0, has_side_effects=True, vmem_limit_bytes=60 * 2**20
+            collective_id=0, has_side_effects=True, vmem_limit_bytes=48 * 2**20
         ),
     )(
-        tokens,
-        group_pos.reshape(8, NG // 8),
-        log_decay.T,
-        in_weight,
-        norm_gain.reshape(1, E),
-        out_weight,
-        inner_gain.reshape(1, D),
-        qkv_weight.transpose(0, 2, 1),
-        attn_out,
+        *(
+            pltpu.with_memory_space_constraint(x, pltpu.HBM)
+            for x in (
+                tokens,
+                group_pos.reshape(8, NG // 8),
+                log_decay.T,
+                in_weight,
+                norm_gain.reshape(1, E),
+                out_weight,
+                inner_gain.reshape(1, D),
+                qkv_weight.transpose(0, 2, 1),
+                attn_out,
+            )
+        )
     )
 
 

time: 58.2 us -> 54.1 us (0.930)
  Pallas kernels: 56.4 us -> 53.2 us
  local copies, waits for them, and re-layouts: 1.67 us -> 0.71 us
    pallas_call x1, Pallas kernels: 56.4 us -> 53.2 us  [shards(): pl.pallas_call(layer, out_shape=jax.ShapeDtypeStruct((TOK, D), BF16), in_...]
    unnamed x1, local copies, waits for them, and re-layouts: 1.67 us -> 0.71 us
where the time goes in v3:
time: 54.1 us; the launch traced here: 53.9 us
  Pallas kernels  53.2 us (98%)
  local copies, waits for them, and re-layouts  0.71 us (1%)
    pallas_call x1, Pallas kernels, shards(): pl.pallas_call(layer, out_shape=jax.ShapeDtypeStruct((TOK, D), BF16), in_...  53.2 us

profile of v3, /device:TPU:1, one launch (start us, length us, event | category | flops | bytes accessed | tf_op | source)
XLA Modules:
  0.0 53.9 jit_solution(7875835648858897385)
XLA Ops:
  0.0 53.2 %shard_map.91 = bf16[256,512]{1,0:T(8,128)(2,1)S(1)} custom-call(bf16[256,512]{1,0:T(8,128)(2,1)} %tokens_h.1, s32[8,128]{1,0:T(8,128)} %bitcast.7, f32[16,256]{1,0:T(8,128)} %bitcast.6, bf16[512,2176]{1,0:T(8,128)(2,1)} %w_in_h.1, f32[1,1024]{1,0:T(1,128)} %bitcast.8, bf16[1024,512]{1,0:T(8,128)(2,1)} %w_out_h.1, f32[1,512]{1,0:T(1,128)} %bitcast.9, ...), custom_call_target="tpu_custom_call" | custom-call | tf_op jit(solution)/shard_map/pallas_call | solution.py:435
  53.2 0.7 %copy.11 = bf16[256,512]{1,0:T(8,128)(2,1)} copy(bf16[256,512]{1,0:T(8,128)(2,1)S(1)} %shard_map.91) | data formatting | bytes 524288

commit v4 on v3

--- a/solution.py
+++ b/solution.py
@@ -179,19 +179,22 @@
         ref = buf.at[block, pl.ds(part * size, size), :]
         return remote(ref, ref, s_sem.at[slot], r_sem.at[parts * block + part], on_ring(hops * way))
 
-    def ring_near(parts, part, way):
-        return (part < parts // 2) == (way == 1)
+    def ring_parts(parts, step):
+        for order in range(parts if step < RING // 2 else parts // 2):
+            for way in (1, -1):
+                yield order, order if way == 1 else (order + parts // 2) % parts, way
 
     def ring_sends(ring, step):
         parts = ring[1]
-        for part in range(parts):
-            for way in (1, -1):
-                block = on_ring(-way * step)
-                slot = part * 2 + (way + 1) // 2
-                copies = [ring_copy(ring, block, part, way, 1, 2 * parts * step + slot)]
-                if step == 2 and ring_near(parts, part, way):
-                    copies.insert(0, ring_copy(ring, block, part, way, 2, 6 * parts + slot))
-                yield part, way, copies
+        for order, part, way in ring_parts(parts, step):
+            block = on_ring(-way * step)
+            slot = part * 2 + (way + 1) // 2
+            copies = []
+            if step == 2 and parts // 4 <= order < parts // 2:
+                copies.append(ring_copy(ring, block, part, way, 2, 6 * parts + slot))
+            if step < 3 or (step == 3 and order < parts // 4):
+                copies.append(ring_copy(ring, block, part, way, 1, 2 * parts * step + slot))
+            yield part, way, copies
 
     def ring_wait(ring, step, part, way):
         ring_copy(ring, on_ring(-way * step), part, way, 1, 0).wait_recv()
@@ -204,18 +207,11 @@
         return (1, -1) if 0 < step < RING // 2 else (1,)
 
     def ring_step(ring, step):
-        parts = ring[1]
-        if step <= 2:
-            for part, way, copies in ring_sends(ring, step):
-                if step > 0:
-                    ring_wait(ring, step, part, way)
-                for copy in copies:
-                    copy.start()
-        else:
-            for part in range(parts):
-                for way in (1, -1):
-                    if step == 3 or ring_near(parts, part, way):
-                        ring_wait(ring, step, part, way)
+        for part, way, copies in ring_sends(ring, step):
+            if step > 0:
+                ring_wait(ring, step, part, way)
+            for copy in copies:
+                copy.start()
         for way in ring_ways(step):
             ring_hand(ring, on_ring(-way * step)).start()
 
@@ -224,7 +220,7 @@
             ring_hand(ring, (on_ring(-way * step) // 2) * 2 + 1 - core).wait_recv()
 
     def ring_done(ring):
-        for step in range(3):
+        for step in range(RING // 2):
             for _, _, copies in ring_sends(ring, step):
                 for copy in copies:
                     copy.wait_send()
@@ -361,6 +357,8 @@
     project(me)
     for step in range(1, RING // 2 + 1):
         ring_step(row_ring, step)
+        if step == 4:
+            ring_step(back_ring, 2)
         ring_sibling_wait(row_ring, step - 1)
         for way in ring_ways(step - 1):
             project((on_ring(-way * (step - 1)) // 2) * 2 + 1 - core)
@@ -368,7 +366,6 @@
             project(on_ring(-way * step))
     ring_sibling_wait(row_ring, RING // 2)
     project((on_ring(RING // 2) // 2) * 2 + 1 - core)
-    ring_step(back_ring, 2)
 
     for p in range(NG // QB):
         packed[p * QB : (p + 1) * QB] = dot(pick[p], qkv[p * QB : p * QB + BAND]).astype(BF16)

time: 54.1 us -> 53.5 us (0.989)
  Pallas kernels: 53.2 us -> 52.6 us
    pallas_call x1, Pallas kernels: 53.2 us -> 52.6 us  [shards(): pl.pallas_call(layer, out_shape=jax.ShapeDtypeStruct((TOK, D), BF16), in_...]
where the time goes in v4:
time: 53.5 us; the launch traced here: 53.3 us
  Pallas kernels  52.6 us (98%)
  local copies, waits for them, and re-layouts  0.71 us (1%)
    pallas_call x1, Pallas kernels, shards(): pl.pallas_call(layer, out_shape=jax.ShapeDtypeStruct((TOK, D), BF16), in_...  52.6 us

profile of v4, /device:TPU:1, one launch (start us, length us, event | category | flops | bytes accessed | tf_op | source)
XLA Modules:
  0.0 53.3 jit_solution(4020454932005666385)
XLA Ops:
  0.0 52.6 %shard_map.91 = bf16[256,512]{1,0:T(8,128)(2,1)S(1)} custom-call(bf16[256,512]{1,0:T(8,128)(2,1)} %tokens_h.1, s32[8,128]{1,0:T(8,128)} %bitcast.7, f32[16,256]{1,0:T(8,128)} %bitcast.6, bf16[512,2176]{1,0:T(8,128)(2,1)} %w_in_h.1, f32[1,1024]{1,0:T(1,128)} %bitcast.8, bf16[1024,512]{1,0:T(8,128)(2,1)} %w_out_h.1, f32[1,512]{1,0:T(1,128)} %bitcast.9, ...), custom_call_target="tpu_custom_call" | custom-call | tf_op jit(solution)/shard_map/pallas_call | solution.py:432
  52.6 0.7 %copy.11 = bf16[256,512]{1,0:T(8,128)(2,1)} copy(bf16[256,512]{1,0:T(8,128)(2,1)S(1)} %shard_map.91) | data formatting | bytes 524288

commit v5 on v4

--- a/solution.py
+++ b/solution.py
@@ -247,8 +247,9 @@
     table = (iota((HEADS, E), 1) // HDIM == iota((HEADS, E), 0)).astype(BF16)
     f_in = spread(jnp.exp(rel), table)
     f_out = spread(jnp.exp(-rel), table)
+    edge = cum[SUB - 1 : SUB]
     few = jnp.concatenate(
-        [mids[0], mids[1], end - mids[0], end - mids[1], mids[1] - mids[0], end, end, end], axis=0
+        [mids[0], mids[1], edge - mids[0], end - mids[1], mids[1] - edge, end - edge, end, end], axis=0
     )
     few = spread(jnp.exp(few), table)
     xs[...] = (proj[:, :E].astype(F32) * f_out).astype(BF16)
@@ -256,7 +257,8 @@
     bmat, cmat = bc[:, :NST], bc[:, NST:]
     low = iota((SUB, SUB), 0) >= iota((SUB, SUB), 1)
     u = [dot_tn(bmat[k * SUB : (k + 1) * SUB], xs[k * SUB : (k + 1) * SUB]) for k in range(2)]
-    local = (u[0] * few[2:3] + u[1] * few[3:4]).astype(BF16)
+    u0 = u[0] * few[2:3]
+    local = (u0 * few[5:6] + u[1] * few[3:4]).astype(BF16)
     for d in range(N):
         r, c = 16 * (d // 4), 256 * (d % 4)
         pieces[d] = local[r : r + 16, c : c + 256]
@@ -291,7 +293,7 @@
     back_to = one_hot.T.astype(BF16)
     put[...] = jnp.concatenate([back_to, back_to], axis=1)
 
-    u0 = (u[0] * few[4:5]).astype(BF16)
+    u0 = (u0 * few[4:5]).astype(BF16)
     for k in range(2):
         b_k, c_k = bmat[k * SUB : (k + 1) * SUB], cmat[k * SUB : (k + 1) * SUB]
         g = jnp.where(low, dot_nt(c_k, b_k), 0.0).astype(BF16)

time: 53.5 us -> 53.5 us (level)
  no operation moved by 1% of the time
where the time goes in v5:
time: 53.5 us; the launch traced here: 53.3 us
  Pallas kernels  52.6 us (98%)
  local copies, waits for them, and re-layouts  0.71 us (1%)
    pallas_call x1, Pallas kernels, shards(): pl.pallas_call(layer, out_shape=jax.ShapeDtypeStruct((TOK, D), BF16), in_...  52.6 us

profile of v5, /device:TPU:1, one launch (start us, length us, event | category | flops | bytes accessed | tf_op | source)
XLA Modules:
  0.0 53.3 jit_solution(9622663988696078829)
XLA Ops:
  0.0 52.6 %shard_map.91 = bf16[256,512]{1,0:T(8,128)(2,1)S(1)} custom-call(bf16[256,512]{1,0:T(8,128)(2,1)} %tokens_h.1, s32[8,128]{1,0:T(8,128)} %bitcast.7, f32[16,256]{1,0:T(8,128)} %bitcast.6, bf16[512,2176]{1,0:T(8,128)(2,1)} %w_in_h.1, f32[1,1024]{1,0:T(1,128)} %bitcast.8, bf16[1024,512]{1,0:T(8,128)(2,1)} %w_out_h.1, f32[1,512]{1,0:T(1,128)} %bitcast.9, ...), custom_call_target="tpu_custom_call" | custom-call | tf_op jit(solution)/shard_map/pallas_call | solution.py:434
  52.6 0.7 %copy.11 = bf16[256,512]{1,0:T(8,128)(2,1)} copy(bf16[256,512]{1,0:T(8,128)(2,1)S(1)} %shard_map.91) | data formatting | bytes 524288
